TPU v7x, 256 devices: a whole 4x4x8 slice. The times are simulated.
256 devices in a mesh: dp: 32 (over y_hi, z, core), fsdp: 8 (over y_lo, x).
Axes of the slice: x: 4, y: 4 (y_hi: 2, y_lo: 2; y = y_hi * 2 + y_lo), z: 8, core: 2. Of those that a mesh axis runs over, the one named last changes fastest.
Arguments:
- feats: bfloat16 [16384, 1792], P(('dp', 'fsdp')), may hold values from -18 to 18
- proj_weight: bfloat16 [1792, 1152], P('fsdp'), may hold values from -0.125 to 0.125
- text_emb: bfloat16 [16384, 1152], P(('dp', 'fsdp')), may hold values from -18 to 18
- partner: int32 [16384], P('dp'), may hold values from 0 to 16383, each once
- log_scale: float32 [1], replicated, may hold values from 0.7 to 1.6
- bias: float32 [1], replicated, may hold values from -3 to -1
Outputs:
- grad_text: float32 [16384, 1152], P(('dp', 'fsdp'))
- grad_feats: bfloat16 [16384, 1792], P(('dp', 'fsdp'))
- grad_weight: float32 [1792, 1152], P('fsdp')
Inputs may be any that keep to these rules, and one draw needn't show every extreme that they name: `partner`: each text matches exactly one image.
All inputs are finite; a program needn't handle non-finite values.
Results may differ from a plain program's by a relative error of at most 0.0064.
Values may be sent and summed in bfloat16 or wider, within the bound.
A program may use at most 64 MiB of HBM per device.

v0:
```python
import functools

import jax
import jax.numpy as jnp
from jax import lax
from jax.experimental import pallas as pl
from jax.experimental.pallas import tpu as pltpu
from jax.sharding import PartitionSpec as P

NORM_EPS = 1e-06
MESH = pl.DeviceIdType.MESH
F32 = jnp.float32
BF16 = jnp.bfloat16
NT = (((1,), (1,)), ((), ()))
STOP = 99


def normalize(values):
    inverse = lax.rsqrt(jnp.sum(values * values, axis=-1, keepdims=True) + NORM_EPS)
    return (values * inverse, inverse)


def kernel(
    zs,
    xs,
    feats,
    wshard,
    text_emb,
    partner,
    log_scale,
    bias,
    grad_text,
    grad_feats,
    grad_weight,
    texts,
    images,
    fsplit,
    fgroup,
    fturned,
    pacc,
    pout,
    pin,
    pmid,
    pin_y,
    pback,
    proj,
    pbuf,
    wbuf,
    tpart,
    tsib,
    image_acc,
    ring_in,
    ring_out,
    yout,
    yin,
    iout,
    iin,
    grads,
    gfout,
    gfin,
    gw,
    gout,
    gsib,
    zout,
    zin,
    gyout,
    gyin,
    fin,
    send,
    recv,
):
    rows, embed = text_emb.shape
    wrows = wshard.shape[0]
    whalf = wrows // 2
    group = 2 * xs
    part_rows = rows // 2
    image_half = group * part_rows
    pair = 2 * rows
    unit = 4 * rows
    half = zs // 2
    p = lax.axis_index("dp")
    f = lax.axis_index("fsdp")
    core = lax.rem(p, 2)
    z = lax.rem(p // 2, zs)
    yh = p // (2 * zs)
    x = lax.rem(f, xs)
    yl = f // xs

    def at_z(zz):
        return (yh * (2 * zs) + zz * 2 + core, f)

    def zplus(by):
        return lax.rem(z + by + zs, zs)

    sib = (p + 1 - 2 * core, f)
    across = (p + 2 * zs * (1 - 2 * yh), f)

    def peer(k):
        dy, dx = k // xs, k % xs
        to_y = 1 - yl if dy else yl
        return to_y * xs + lax.rem(x + dx, xs)

    used = [0]
    pending = []

    def ids(count):
        first = used[0]
        used[0] += count
        return first

    def copy(src, dst, i, device):
        return pltpu.make_async_remote_copy(
            src_ref=src,
            dst_ref=dst,
            send_sem=send.at[i],
            recv_sem=recv.at[i],
            device_id=device,
            device_id_type=MESH,
        )

    def start(src, dst, i, device):
        c = copy(src, dst, i, device)
        c.start()
        pending.append(c)
        return c

    group_ks = [k for k in (1, xs - 1, xs, 2, xs + 1, 2 * xs - 1, xs + 2) if k < group]
    group_ks = list(dict.fromkeys(group_ks))
    assert len(group_ks) == group - 1

    def to_group(src, dst):
        first = ids(group)
        return [start(src(k), dst(k), first + k, (p, peer(k))) for k in group_ks]

    def wait_all(copies):
        for c in copies:
            c.wait_recv()

    dxs = list(dict.fromkeys([1, xs - 1] + list(range(2, xs - 1))))
    facing = (1 - yl) * xs + x

    def along_x(dx):
        return yl * xs + lax.rem(x + dx + xs, xs)

    def facing_x(dx):
        return (1 - yl) * xs + lax.rem(x + dx + xs, xs)

    def gather_start(buf, h):
        own = buf.at[h, f]
        cy = start(own, own, ids(1), (p, facing))
        return cy, [start(own, own, ids(1), (p, along_x(dx))) for dx in dxs]

    def gather_x_first(buf, h, copies):
        cy, cx = copies
        out = [cy]
        for dx, c in zip(dxs, cx):
            c.wait_recv()
            a = buf.at[h, along_x(-dx)]
            out.append(start(a, a, ids(1), (p, facing)))
        return out

    def gather_y_first(buf, h, copies):
        cy, cx = copies
        cy.wait_recv()
        a = buf.at[h, facing]
        return cx + [start(a, a, ids(1), (p, along_x(dx))) for dx in dxs]

    barrier = pltpu.get_barrier_semaphore()
    others = [sib, across]
    others += [at_z(zplus(k)) for k in range(1, zs)]
    others += [(p, peer(k)) for k in range(1, group)]
    for device in others:
        pl.semaphore_signal(barrier, inc=1, device_id=device, device_id_type=MESH)

    fsplit[...] = jnp.zeros_like(fsplit)
    gfout[...] = jnp.zeros_like(gfout)
    for j in range(group):
        fsplit[j, :, :wrows] = feats[:, j * wrows : (j + 1) * wrows]
    text_unit, text_inv = normalize(text_emb[...].astype(F32))

    def chunk(q):
        y = yh if q == 0 else 1 - yh
        return pl.ds(pl.multiple_of(core * pair + y * rows, 16), rows)

    texts[z, chunk(0)] = text_unit.astype(BF16)
    fgroup[f] = fsplit[f]
    for h in range(2):
        for j in range(group):
            lane = j * rows + h * part_rows
            pbuf[h, :, j * part_rows : (j + 1) * part_rows] = partner[:, lane : lane + part_rows]
    image_acc[...] = jnp.zeros_like(image_acc)
    pl.semaphore_wait(barrier, len(others))

    fcopies = to_group(lambda k: fsplit.at[peer(k)], lambda k: fgroup.at[f])

    own_text = texts.at[z, chunk(0)]
    ty = start(own_text, own_text, ids(1), across)
    ring = {}
    text_sib = {}

    def ring_send(way, s, q):
        u = zplus(-way * s)
        a = texts.at[u, chunk(q)]
        ring[way, s, q] = start(a, a, ids(1), at_z(zplus(way)))

    def to_sib(by, q):
        a = texts.at[zplus(by), chunk(q)]
        text_sib.setdefault(by, []).append(start(a, a, ids(1), sib))

    def arrive(s, q):
        for way in (1, -1):
            if (way, s, q) not in ring:
                continue
            ring[way, s, q].wait_recv()
            if s < half - 2 or (s == half - 2 and q == (0 if way == 1 else 1)):
                ring_send(way, s + 1, q)
            by = -way * (s + 1)
            to_sib(half if by == -half else by, q)

    def text_ready(by):
        wait_all(text_sib[by])

    ring_send(1, 0, 0)
    ring_send(-1, 0, 0)
    to_sib(0, 0)

    wait_all(fcopies)
    pcopies = []

    def own_block(ref, h, j):
        return ref[h, pl.ds(pl.multiple_of(j * part_rows, 16), part_rows)]

    def sums_start_x():
        relay = [start(pout.at[0, facing_x(dx)], pmid.at[i], ids(1), (p, along_x(dx))) for i, dx in enumerate(dxs)]
        final = [start(pout.at[0, along_x(dx)], pin.at[0, i], ids(1), (p, along_x(dx))) for i, dx in enumerate(dxs)]
        return relay, final

    def sums_start_y():
        return [start(pout.at[1, facing_x(dx)], pin_y.at[i], ids(1), (p, facing)) for i, dx in enumerate(dxs + [0])]

    for h in range(2):
        cols = fgroup[:, h * part_rows : (h + 1) * part_rows, :wrows].reshape(image_half, wrows)
        pacc[h] = jnp.dot(cols, wshard[...], preferred_element_type=F32)
        pout[h] = pacc[h].reshape(group, part_rows, embed).astype(BF16)
        pcopies.append(sums_start_y() if h else sums_start_x())
        if h == 0:
            arrive(0, 0)
    ty.wait_recv()
    ring_send(1, 0, 1)
    ring_send(-1, 0, 1)
    to_sib(0, 1)
    arrive(1, 0)
    for h in range(2):
        cols = fgroup[:, h * part_rows : (h + 1) * part_rows, :wrows].reshape(image_half, wrows)
        fturned[h] = cols.T
    relay, final0 = pcopies[0]
    wait_all(relay)
    total = own_block(pacc, 0, facing)
    for i in range(len(dxs)):
        total += pmid[i].astype(F32)
    pback[0] = total.astype(BF16)
    final0.append(start(pback.at[0], pin.at[0, len(dxs)], ids(1), (p, facing)))
    arrive(0, 1)
    final1 = []
    for i, dx in enumerate(dxs):
        pcopies[1][i].wait_recv()
        pback[1 + i] = (own_block(pacc, 1, along_x(dx)) + pin_y[i].astype(F32)).astype(BF16)
        final1.append(start(pback.at[1 + i], pin.at[1, i], ids(1), (p, along_x(dx))))

    def project(h, copies):
        total = own_block(pacc, h, f)
        wait_all(copies)
        if h:
            pcopies[1][len(dxs)].wait_recv()
            total += pin_y[len(dxs)].astype(F32)
        for i in range(len(copies)):
            total += pin[h, i].astype(F32)
        proj[h] = total
        images[h, f] = normalize(total)[0].astype(BF16)
        return gather_start(images, h)

    first = project(0, final0)
    arrive(2, 0)
    second_half = project(1, final1)
    arrive(1, 1)
    icopies = [gather_x_first(images, 0, first)]
    icopies.append(gather_y_first(images, 1, second_half))
    arrive(3, 0)
    arrive(2, 1)

    scale = jnp.exp(log_scale[...])
    half_scale = 0.5 * scale
    half_shift = 0.5 * bias[...]

    def weigh(u, h, block):
        image_rows = images[h].reshape(image_half, embed)
        dots = lax.dot_general(block, image_rows, NT, preferred_element_type=F32)
        r = lax.broadcasted_iota(jnp.int32, (unit, 1), 0)
        c_of = r // pair
        y_of = lax.rem(r // rows, 2)
        index = ((y_of * (2 * zs) + u * 2 + c_of) * group + f) * rows + lax.rem(r, rows)
        level = jnp.where(pbuf[h] == index, F32(-0.5), F32(0.5))
        weight = (0.5 * jnp.tanh(half_scale * dots + half_shift) + level).astype(BF16)
        wbuf[u, :, h * image_half : (h + 1) * image_half] = weight
        return weight

    def front(units, h):
        blocks = [texts[u] for u in units]
        weights = [weigh(u, h, block) for u, block in zip(units, blocks)]
        total = jnp.dot(weights[0].T, blocks[0], preferred_element_type=F32)
        for weight, block in zip(weights[1:], blocks[1:]):
            total += jnp.dot(weight.T, block, preferred_element_type=F32)
        image_acc[h] += total

    iscopies = []

    def image_sums(h):
        iout[h] = image_acc[h].reshape(group, part_rows, embed).astype(BF16)
        iscopies.append(to_group(lambda k: iout.at[h, peer(k)], lambda k: iin.at[h, k]))

    text_ready(0)
    wait_all(icopies[0])
    front([z], 0)
    for s in range(1, half):
        if s == half - 1:
            arrive(s, 1)
        text_ready(-s)
        text_ready(s)
        front([zplus(-s), zplus(s)], 0)
    text_ready(half)
    front([zplus(half)], 0)
    image_sums(0)
    wait_all(icopies[1])

    def second(i, carry):
        front([2 * i, 2 * i + 1], 1)
        return carry

    lax.fori_loop(0, zs // 2, second, 0)
    image_sums(1)

    tpid = ids(zs)
    sib_pair = pl.ds(pl.multiple_of((1 - core) * pair, 16), pair)

    def part_copy(k):
        return copy(tpart.at[k, sib_pair], tsib.at[k], tpid + k, sib)

    def back(k, carry):
        d = half - (k + 1) // 2
        u = lax.rem(z + jnp.where(lax.rem(k, 2) == 1, d, zs - d), zs)
        image_rows = images[...].reshape(2 * image_half, embed)
        tpart[k] = jnp.dot(wbuf[u], image_rows, preferred_element_type=F32).astype(BF16)
        part_copy(k).start()
        return carry

    rsid, lsid = ids(half), ids(half)
    sum_r, sum_l = [], []

    def own_sum(k, lo, count):
        at = pl.ds(pl.multiple_of(core * pair + lo, 16), count)
        return tpart[k, at].astype(F32) + tsib[k, lo : lo + count].astype(F32)

    def sum_step(s):
        kr, kl = (0, 0) if s == 0 else (2 * s - 1, 2 * s)
        for k in range(0 if s == 0 else kr, kl + 1):
            part_copy(k).wait_recv()
        if s:
            sum_r[s - 1].wait_recv()
            sum_l[s - 1].wait_recv()
        if s == 0:
            ring_out[0, 0, :rows] = own_sum(0, 0, rows).astype(BF16)
            ring_out[1, 0, rows:] = own_sum(0, rows, rows).astype(BF16)
            a, b = pl.ds(0, rows), pl.ds(rows, rows)
        elif s == 1:
            ring_out[0, 1, :rows] = (own_sum(kr, 0, rows) + ring_in[0, 0, :rows].astype(F32)).astype(BF16)
            ring_out[0, 1, rows:] = own_sum(kr, rows, rows).astype(BF16)
            ring_out[1, 1, :rows] = own_sum(kl, 0, rows).astype(BF16)
            ring_out[1, 1, rows:] = (own_sum(kl, rows, rows) + ring_in[1, 0, rows:].astype(F32)).astype(BF16)
            a = b = pl.ds(0, pair)
        else:
            ring_out[0, s] = (own_sum(kr, 0, pair) + ring_in[0, s - 1].astype(F32)).astype(BF16)
            ring_out[1, s] = (own_sum(kl, 0, pair) + ring_in[1, s - 1].astype(F32)).astype(BF16)
            a = b = pl.ds(0, pair)
        sum_r.append(start(ring_out.at[0, s, a], ring_in.at[0, s, a], rsid + s, at_z(zplus(1))))
        sum_l.append(start(ring_out.at[1, s, b], ring_in.at[1, s, b], lsid + s, at_z(zplus(-1))))

    lax.fori_loop(0, 2, back, 0)
    sum_step(0)
    lax.fori_loop(2, zs, back, 0, unroll=2)


    def project_back(h):
        total = own_block(image_acc, h, f)
        wait_all(iscopies[h])
        for k in group_ks:
            total += iin[h, k].astype(F32)
        image_dir = scale * total
        image_unit, image_inv = normalize(proj[h])
        along = jnp.sum(image_unit * image_dir, axis=-1, keepdims=True)
        grads[h, f] = (image_inv * (image_dir - image_unit * along)).astype(BF16)
        return gather_start(grads, h)

    first = project_back(0)
    sum_step(1)
    second_half = project_back(1)
    gcopies = [gather_x_first(grads, 0, first)]
    gcopies.append(gather_y_first(grads, 1, second_half))
    sum_step(2)

    own_half = pl.ds(pl.multiple_of(core * whalf, 16), whalf)
    other_half = pl.ds(pl.multiple_of((1 - core) * whalf, 16), whalf)
    part = zout.shape[1]
    used_parts = whalf // part
    for j in range(used_parts, zs):
        zout[j] = jnp.zeros_like(zout[j])
    middle = (embed // 128 + 1) // 2 * 128
    cuts = [slice(0, middle), slice(middle, embed)]

    def weight_part(h, at, cut):
        some = grads[h, :, :, cut].reshape(image_half, cut.stop - cut.start)
        return jnp.dot(fturned[h, at], some, preferred_element_type=F32)

    wait_all(gcopies[0])
    for cut in cuts:
        gw[0, :, cut] = weight_part(0, other_half, cut)
        gw[1, :, cut] = weight_part(0, own_half, cut)
    wait_all(gcopies[1])
    gs = []
    for cut in cuts:
        gout[:, cut] = (gw[0, :, cut] + weight_part(1, other_half, cut)).astype(BF16)
        gs.append(start(gout.at[:, cut], gsib.at[:, cut], ids(1), sib))
        gw[1, :, cut] += weight_part(1, own_half, cut)
    zcopies = []
    for cut, c in zip(cuts, gs):
        c.wait_recv()
        total = (gw[1, :, cut] + gsib[:, cut].astype(F32)).astype(BF16)
        zout[:used_parts, :, cut] = total.reshape(used_parts, part, cut.stop - cut.start)
        zcopies.append(
            [
                start(zout.at[zplus(k), :, cut], zin.at[k, :, cut], ids(1), at_z(zplus(k)))
                for k in range(1, zs)
            ]
        )

    gfcopies = []
    for h in range(2):
        cols = lax.dot_general(
            grads[h].reshape(image_half, embed), wshard[...], NT, preferred_element_type=F32
        )
        gfout[h, :, :, :wrows] = cols.astype(BF16).reshape(group, part_rows, wrows)
        gfcopies += to_group(lambda k: gfout.at[h, peer(k)], lambda k: gfin.at[h, f])
        gfin[h, f] = gfout[h, f]
    for s in range(3, half):
        sum_step(s)

    gy = []
    for cut, copies in zip(cuts, zcopies):
        weight_sum = zout[z, :, cut].astype(F32)
        for k, c in zip(range(1, zs), copies):
            c.wait_recv()
            weight_sum += zin[k, :, cut].astype(F32)
        gyout[:, cut] = weight_sum.astype(BF16)
        gy.append(start(gyout.at[:, cut], gyin.at[:, cut], ids(1), across))
    fincopies = []
    for cut, c in zip(cuts, gy):
        c.wait_recv()
        fin[core, z, :, cut] = (
            gyout[:, cut].astype(F32) + gyin[:, cut].astype(F32)
        ).astype(BF16)
        own = fin.at[core, z, :, cut]
        fincopies.append([start(own, own, ids(1), at_z(zplus(k))) for k in range(1, zs)])
    wait_all(gfcopies)
    for h in range(2):
        for j in range(group):
            at = (slice(h * part_rows, (h + 1) * part_rows), slice(j * wrows, (j + 1) * wrows))
            grad_feats[at] = gfin[h, j, :, :wrows]

    part_copy(zs - 1).wait_recv()
    sum_r[half - 1].wait_recv()
    sum_l[half - 1].wait_recv()
    theirs = pl.ds(pl.multiple_of((1 - yh) * rows, 16), rows)
    ours = pl.ds(pl.multiple_of(yh * rows, 16), rows)

    def gathered(at, lo):
        here = pl.ds(pl.multiple_of(core * pair + lo, 16), rows)
        return (
            (tpart[zs - 1, here].astype(F32) + tsib[zs - 1, at].astype(F32))
            + (ring_in[0, half - 1, at].astype(F32) + ring_in[1, half - 1, at].astype(F32))
        )

    yout[...] = gathered(theirs, (1 - yh) * rows).astype(BF16)
    yc = start(yout, yin, ids(1), across)
    fs = []
    for cut, copies in zip(cuts, fincopies):
        wait_all(copies)
        own = fin.at[core, :, :, cut]
        fs.append(start(own, own, ids(1), sib))
    yc.wait_recv()
    text_dir = scale * (gathered(ours, yh * rows) + yin[...].astype(F32))
    text_unit, text_inv = normalize(text_emb[...].astype(F32))
    along = jnp.sum(text_unit * text_dir, axis=-1, keepdims=True)
    grad_text[...] = text_inv * (text_dir - text_unit * along)
    wait_all(fs)
    for c in range(2):
        grad_weight[c * whalf : (c + 1) * whalf] = (
            fin[c, :used_parts].reshape(whalf, embed)
        )

    for c in pending:
        c.wait_send()

    def part_done(k, carry):
        part_copy(k).wait_send()
        return carry

    lax.fori_loop(0, zs, part_done, 0)


SEMS = 224


def move(a, b, c, x, y, z):
    z[...] = c[...].astype(F32)
    x[...] = a[...]
    y[...] = b[...]


def body(zs, xs, feats, proj_weight, text_emb, partner, log_scale, bias):
    rows, width = feats.shape
    wrows, embed = proj_weight.shape
    group = 2 * xs
    pair, unit = 2 * rows, 4 * rows
    half = zs // 2
    whalf = wrows // 2
    part_rows = rows // 2
    image_half = group * part_rows
    lanes = -(-wrows // 128) * 128
    part = -(-whalf // zs // 16) * 16
    vmem = pl.BlockSpec(memory_space=pltpu.VMEM)
    halves = ((2, group, part_rows, embed), BF16)
    scratch = [
        ((zs, unit, embed), BF16),
        halves,
        ((group, rows, lanes), BF16),
        ((group, rows, lanes), BF16),
        ((2, wrows, image_half), BF16),
        ((2, image_half, embed), F32),
        halves,
        ((2, group // 2, part_rows, embed), BF16),
        ((group // 2, part_rows, embed), BF16),
        ((group // 2, part_rows, embed), BF16),
        ((group // 2, part_rows, embed), BF16),
        ((2, part_rows, embed), F32),
        ((2, 1, image_half), jnp.int32),
        ((zs, unit, 2 * image_half), BF16),
        ((zs, unit, embed), BF16),
        ((zs, pair, embed), BF16),
        ((2, image_half, embed), F32),
        ((2, half, pair, embed), BF16),
        ((2, half, pair, embed), BF16),
        ((rows, embed), BF16),
        ((rows, embed), BF16),
        halves,
        halves,
        halves,
        ((2, group, part_rows, lanes), BF16),
        ((2, group, part_rows, lanes), BF16),
        ((2, whalf, embed), F32),
        ((whalf, embed), BF16),
        ((whalf, embed), BF16),
        ((zs, part, embed), BF16),
        ((zs, part, embed), BF16),
        ((part, embed), BF16),
        ((part, embed), BF16),
        ((2, zs, part, embed), BF16),
    ]
    shapes = (
        jax.ShapeDtypeStruct((rows, embed), F32),
        jax.ShapeDtypeStruct((rows, width), BF16),
        jax.ShapeDtypeStruct((wrows, embed), BF16),
    )
    outs = pl.pallas_call(
        functools.partial(kernel, zs, xs),
        out_shape=shapes,
        in_specs=[vmem] * 6,
        out_specs=(vmem,) * 3,
        scratch_shapes=[pltpu.VMEM(shape, kind) for shape, kind in scratch]
        + [pltpu.SemaphoreType.DMA((SEMS,)), pltpu.SemaphoreType.DMA((SEMS,))],
        compiler_params=pltpu.CompilerParams(
            collective_id=0, has_side_effects=True, vmem_limit_bytes=56 * 2**20
        ),
    )(
        feats,
        proj_weight,
        text_emb,
        partner.reshape(1, group * rows),
        log_scale.reshape(1, 1),
        bias.reshape(1, 1),
    )
    return pl.pallas_call(
        move,
        out_shape=shapes[:2] + (jax.ShapeDtypeStruct((wrows, embed), F32),),
        in_specs=[vmem] * 3,
        out_specs=(vmem,) * 3,
    )(*outs)


def solution(mesh):
    zs = mesh.shape["dp"] // 4
    xs = mesh.shape["fsdp"] // 2
    return jax.shard_map(
        functools.partial(body, zs, xs),
        mesh=mesh,
        in_specs=(
            P(("dp", "fsdp"), None),
            P("fsdp", None),
            P(("dp", "fsdp"), None),
            P("dp"),
            P(),
            P(),
        ),
        out_specs=(P(("dp", "fsdp"), None), P(("dp", "fsdp"), None), P("fsdp", None)),
        check_vma=False,
    )
```

profile of v0, /device:TPU:1, one launch (start us, length us, event | category | flops | bytes accessed | tf_op | source)
XLA Modules:
  0.0 105.1 jit_solution(16921466663169522892)
XLA Ops:
  1.9 100.7 %shard_map.85 = (f32[64,1152]{1,0:T(8,128)}, bf16[64,1792]{1,0:T(8,128)(2,1)}, bf16[224,1152]{1,0:T(8,128)(2,1)}) custom-call(bf16[64,1792]{1,0:T(8,128)(2,1)} %feats.1, bf16[224,1152]{1,0:T(8,128)(2,1)} %wshard.1, bf16[64,1152]{1,0:T(8,128)(2,1)} %text_emb.1, s32[1,512]{1,0:T(1,128)} %bitcast.5, f32[1,1]{1,0:T(1,128)} %bitcast.3.log_scale, f32[1,1]{1,0:T(1,128)} %bitcast.4.bias), custom_call_target="tpu_custom_call" | custom-call | tf_op jit(solution)/shard_map/pallas_call | solution.py:582
  102.7 2.4 %shard_map.86 = (f32[64,1152]{1,0:T(8,128)}, bf16[64,1792]{1,0:T(8,128)(2,1)}, f32[224,1152]{1,0:T(8,128)}) custom-call(f32[64,1152]{1,0:T(8,128)} %get-tuple-element.6.a, bf16[64,1792]{1,0:T(8,128)(2,1)} %get-tuple-element.7.b, bf16[224,1152]{1,0:T(8,128)(2,1)} %get-tuple-element.8.c), custom_call_target="tpu_custom_call" | custom-call | tf_op jit(solution)/shard_map/pallas_call | solution.py:600
where the time goes:
time: 105 us
  Pallas kernels  103 us (98%)
  between operations  1.93 us (2%)
    pallas_call x1, Pallas kernels, body(): pl.pallas_call(functools.partial(kernel, zs, xs), out_shape=shapes, in_sp...  101 us
    pallas_call x1, Pallas kernels, body(): pl.pallas_call(move, out_shape=shapes[:2] + (jax.ShapeDtypeStruct((wrows,...  2.41 us

commit v1 on v0

--- a/solution.py
+++ b/solution.py
@@ -23,12 +23,18 @@
 def kernel(
     zs,
     xs,
+    feats_in,
+    wshard_in,
+    text_in,
+    partner,
+    log_scale,
+    bias,
+    grad_text_out,
+    grad_feats_out,
+    grad_weight_out,
     feats,
     wshard,
     text_emb,
-    partner,
-    log_scale,
-    bias,
     grad_text,
     grad_feats,
     grad_weight,
@@ -68,6 +74,7 @@
     fin,
     send,
     recv,
+    local,
 ):
     rows, embed = text_emb.shape
     wrows = wshard.shape[0]
@@ -165,6 +172,12 @@
         a = buf.at[h, facing]
         return cx + [start(a, a, ids(1), (p, along_x(dx))) for dx in dxs]
 
+    feats_load = pltpu.make_async_copy(feats_in, feats, local.at[0])
+    text_load = pltpu.make_async_copy(text_in, text_emb, local.at[1])
+    weight_load = pltpu.make_async_copy(wshard_in, wshard, local.at[2])
+    for c in (feats_load, text_load, weight_load):
+        c.start()
+
     barrier = pltpu.get_barrier_semaphore()
     others = [sib, across]
     others += [at_z(zplus(k)) for k in range(1, zs)]
@@ -172,10 +185,14 @@
     for device in others:
         pl.semaphore_signal(barrier, inc=1, device_id=device, device_id_type=MESH)
 
+    feats_load.wait()
     fsplit[...] = jnp.zeros_like(fsplit)
-    gfout[...] = jnp.zeros_like(gfout)
     for j in range(group):
         fsplit[j, :, :wrows] = feats[:, j * wrows : (j + 1) * wrows]
+    pl.semaphore_wait(barrier, len(others))
+    fcopies = to_group(lambda k: fsplit.at[peer(k)], lambda k: fgroup.at[f])
+
+    text_load.wait()
     text_unit, text_inv = normalize(text_emb[...].astype(F32))
 
     def chunk(q):
@@ -183,16 +200,6 @@
         return pl.ds(pl.multiple_of(core * pair + y * rows, 16), rows)
 
     texts[z, chunk(0)] = text_unit.astype(BF16)
-    fgroup[f] = fsplit[f]
-    for h in range(2):
-        for j in range(group):
-            lane = j * rows + h * part_rows
-            pbuf[h, :, j * part_rows : (j + 1) * part_rows] = partner[:, lane : lane + part_rows]
-    image_acc[...] = jnp.zeros_like(image_acc)
-    pl.semaphore_wait(barrier, len(others))
-
-    fcopies = to_group(lambda k: fsplit.at[peer(k)], lambda k: fgroup.at[f])
-
     own_text = texts.at[z, chunk(0)]
     ty = start(own_text, own_text, ids(1), across)
     ring = {}
@@ -224,6 +231,15 @@
     ring_send(-1, 0, 0)
     to_sib(0, 0)
 
+    fgroup[f] = fsplit[f]
+    gfout[...] = jnp.zeros_like(gfout)
+    for h in range(2):
+        for j in range(group):
+            lane = j * rows + h * part_rows
+            pbuf[h, :, j * part_rows : (j + 1) * part_rows] = partner[:, lane : lane + part_rows]
+    image_acc[...] = jnp.zeros_like(image_acc)
+
+    weight_load.wait()
     wait_all(fcopies)
     pcopies = []
 
@@ -474,6 +490,8 @@
         for j in range(group):
             at = (slice(h * part_rows, (h + 1) * part_rows), slice(j * wrows, (j + 1) * wrows))
             grad_feats[at] = gfin[h, j, :, :wrows]
+    feats_store = pltpu.make_async_copy(grad_feats, grad_feats_out, local.at[0])
+    feats_store.start()
 
     part_copy(zs - 1).wait_recv()
     sum_r[half - 1].wait_recv()
@@ -500,11 +518,15 @@
     text_unit, text_inv = normalize(text_emb[...].astype(F32))
     along = jnp.sum(text_unit * text_dir, axis=-1, keepdims=True)
     grad_text[...] = text_inv * (text_dir - text_unit * along)
+    text_store = pltpu.make_async_copy(grad_text, grad_text_out, local.at[1])
+    text_store.start()
     wait_all(fs)
     for c in range(2):
         grad_weight[c * whalf : (c + 1) * whalf] = (
             fin[c, :used_parts].reshape(whalf, embed)
         )
+    weight_store = pltpu.make_async_copy(grad_weight, grad_weight_out, local.at[2])
+    weight_store.start()
 
     for c in pending:
         c.wait_send()
@@ -514,6 +536,9 @@
         return carry
 
     lax.fori_loop(0, zs, part_done, 0)
+    feats_store.wait()
+    text_store.wait()
+    weight_store.wait()
 
 
 SEMS = 224
@@ -537,8 +562,15 @@
     lanes = -(-wrows // 128) * 128
     part = -(-whalf // zs // 16) * 16
     vmem = pl.BlockSpec(memory_space=pltpu.VMEM)
+    anywhere = pl.BlockSpec(memory_space=pl.ANY)
     halves = ((2, group, part_rows, embed), BF16)
     scratch = [
+        ((rows, width), BF16),
+        ((wrows, embed), BF16),
+        ((rows, embed), BF16),
+        ((rows, embed), F32),
+        ((rows, width), BF16),
+        ((wrows, embed), BF16),
         ((zs, unit, embed), BF16),
         halves,
         ((group, rows, lanes), BF16),
@@ -582,10 +614,10 @@
     outs = pl.pallas_call(
         functools.partial(kernel, zs, xs),
         out_shape=shapes,
-        in_specs=[vmem] * 6,
-        out_specs=(vmem,) * 3,
+        in_specs=[anywhere] * 3 + [vmem] * 3,
+        out_specs=(anywhere,) * 3,
         scratch_shapes=[pltpu.VMEM(shape, kind) for shape, kind in scratch]
-        + [pltpu.SemaphoreType.DMA((SEMS,)), pltpu.SemaphoreType.DMA((SEMS,))],
+        + [pltpu.SemaphoreType.DMA((SEMS,)), pltpu.SemaphoreType.DMA((SEMS,)), pltpu.SemaphoreType.DMA((3,))],
         compiler_params=pltpu.CompilerParams(
             collective_id=0, has_side_effects=True, vmem_limit_bytes=56 * 2**20
         ),

time: 105 us -> 104 us (level)
  no operation moved by 1% of the time
where the time goes in v1:
time: 104 us
  Pallas kernels  102 us (98%)
  between operations  1.93 us (2%)
    pallas_call x1, Pallas kernels, body(): pl.pallas_call(functools.partial(kernel, zs, xs), out_shape=shapes, in_sp...  99.7 us
    pallas_call x1, Pallas kernels, body(): pl.pallas_call(move, out_shape=shapes[:2] + (jax.ShapeDtypeStruct((wrows,...  2.41 us

profile of v1, /device:TPU:1, one launch (start us, length us, event | category | flops | bytes accessed | tf_op | source)
XLA Modules:
  0.0 104.1 jit_solution(11052861943553531555)
XLA Ops:
  1.9 99.7 %shard_map.85 = (f32[64,1152]{1,0:T(8,128)}, bf16[64,1792]{1,0:T(8,128)(2,1)}, bf16[224,1152]{1,0:T(8,128)(2,1)}) custom-call(bf16[64,1792]{1,0:T(8,128)(2,1)} %feats_in.1, bf16[224,1152]{1,0:T(8,128)(2,1)} %wshard_in.1, bf16[64,1152]{1,0:T(8,128)(2,1)} %text_in.1, s32[1,512]{1,0:T(1,128)} %bitcast.5, f32[1,1]{1,0:T(1,128)} %bitcast.3.log_scale, ...), custom_call_target="tpu_custom_call" | custom-call | tf_op jit(solution)/shard_map/pallas_call | solution.py:614
  101.6 2.4 %shard_map.86 = (f32[64,1152]{1,0:T(8,128)}, bf16[64,1792]{1,0:T(8,128)(2,1)}, f32[224,1152]{1,0:T(8,128)}) custom-call(f32[64,1152]{1,0:T(8,128)} %get-tuple-element.6.a, bf16[64,1792]{1,0:T(8,128)(2,1)} %get-tuple-element.7.b, bf16[224,1152]{1,0:T(8,128)(2,1)} %get-tuple-element.8.c), custom_call_target="tpu_custom_call" | custom-call | tf_op jit(solution)/shard_map/pallas_call | solution.py:632
